TPU v7x, 32 devices: a whole 2x2x4 slice. The times are simulated.
32 devices in a mesh: gx: 4 (over z), gy: 8 (over y, x, core).
Axes of the slice: x: 2, y: 2, z: 4, core: 2. Of those that a mesh axis runs over, the one named last changes fastest.
Arguments:
- face_pieces: bfloat16 [4, 8, 4, 384, 512], P('gx', 'gy'), may hold values from -6 to 6
- edge_pieces: bfloat16 [4, 8, 4, 128, 512], P('gx', 'gy'), may hold values from -6 to 6
- face_counts: int32 [4, 8, 4], P('gx', 'gy'), may hold values from 0 to 6, as said below
- edge_counts: int32 [4, 8, 4], P('gx', 'gy'), may hold values from 0 to 2, as said below
- schur_inv: bfloat16 [4, 8, 2048, 2048], P('gx', 'gy'), may hold values from -0.125 to 0.125
- coarse_basis: bfloat16 [4, 8, 2048, 128], P('gx', 'gy'), may hold values from -0.125 to 0.125
- coarse_mat: float32 [4, 8, 128, 128], P('gx', 'gy'), as said below
- lift_one: float32 [4, 8, 128, 128], P('gx', 'gy'), as said below
- lift_two: float32 [4, 8, 128, 128], P('gx', 'gy'), as said below
Outputs:
- preconditioned_faces: bfloat16 [4, 8, 4, 384, 512], P('gx', 'gy')
- preconditioned_edges: bfloat16 [4, 8, 4, 128, 512], P('gx', 'gy')
Inputs may be any that keep to these rules, and one draw needn't show every extreme that they name: face_counts[i, j, k] is the number of live 64-row blocks in face slot k; it is equal at both owners of the face, 0 exactly where an owner lies outside the grid, and 6 is reached in every draw. edge_counts[i, j, k] is the number of live 64-row blocks in edge slot k; it is equal at all four owners of the edge, 0 exactly where some owner lies outside the grid, and 2 is reached in every draw. `coarse_mat`: every block is symmetric positive definite. `lift_one`: every block is nonsingular. `lift_two`: every block is nonsingular, and the blocks of subdomains (i, 2m) and (i, 2m + 1) are equal.
All inputs are finite; a program needn't handle non-finite values.
Results may differ from a plain program's by a relative error of at most 0.0062.
Values may be sent and summed in bfloat16 or wider, within the bound.
A program may use at most 128 MiB of HBM per device.

v0:
```python
import jax
import jax.numpy as jnp
from jax import lax
from jax.sharding import PartitionSpec as P

ROWS = 64


def from_behind(value, axis, steps):
    count = lax.axis_size(axis)
    first, last = (max(0, -steps), min(count, count - steps))
    return lax.ppermute(value, axis, [(source, source + steps) for source in range(first, last)])


def from_partner(value, axis, apart):
    mask = 2**apart
    pairs = [(source, source ^ mask) for source in range(lax.axis_size(axis))]
    return lax.ppermute(value, axis, pairs)


def widen(values):
    return values.astype(jnp.float32)


def neighbour_sum(faces, edges):
    row_faces = {}
    for offset, source in ((1, 3), (-1, 0)):
        row_faces[offset] = from_behind(faces[source], "gx", offset)
    col_faces = {}
    for offset, source in ((1, 2), (-1, 1)):
        col_faces[offset] = from_behind(faces[source], "gy", offset)
    row_edges = {}
    for offset, first in ((1, 2), (-1, 0)):
        row_edges[offset] = from_behind(edges[first : first + 2], "gx", offset)
    col_edges = {}
    for offset, first_edge, second_edge in ((1, 1, 3), (-1, 0, 2)):
        col_edges[offset] = from_behind(
            jnp.stack([edges[first_edge], edges[second_edge]]), "gy", offset
        )
    corners = {}
    for offset, member in ((1, 1), (-1, 0)):
        corners[offset] = from_behind(
            jnp.stack([row_edges[1][member], row_edges[-1][member]]), "gy", offset
        )
    north = row_faces[1]
    south = row_faces[-1]
    west = col_faces[1]
    east = col_faces[-1]
    above = (row_edges[1][0], row_edges[1][1])
    below = (row_edges[-1][0], row_edges[-1][1])
    left = (col_edges[1][0], col_edges[1][1])
    right = (col_edges[-1][0], col_edges[-1][1])
    diag_left = (corners[1][0], corners[1][1])
    diag_right = (corners[-1][0], corners[-1][1])
    face_total = widen(faces) + jnp.stack([widen(north), widen(west), widen(east), widen(south)])
    north_west = widen(edges[0]) + widen(left[0]) + widen(above[0]) + widen(diag_left[0])
    north_east = widen(edges[1]) + widen(right[0]) + widen(above[1]) + widen(diag_right[0])
    south_west = widen(edges[2]) + widen(left[1]) + widen(below[0]) + widen(diag_left[1])
    south_east = widen(edges[3]) + widen(right[1]) + widen(below[1]) + widen(diag_right[1])
    return (face_total, jnp.stack([north_west, north_east, south_west, south_east]))


def body(
    face_pieces,
    edge_pieces,
    face_counts,
    edge_counts,
    schur_inv,
    coarse_basis,
    coarse_mat,
    lift_one,
    lift_two,
):
    highest = lax.Precision.HIGHEST
    contract_first = (((0,), (0,)), ((), ()))
    faces = face_pieces[0, 0]
    edges = edge_pieces[0, 0]
    face_len = faces.shape[1]
    edge_len = edges.shape[1]
    vectors = faces.shape[2]
    face_live = (
        lax.broadcasted_iota(jnp.int32, (4, face_len, 1), 1)
        < (face_counts[0, 0] * ROWS)[:, None, None]
    ).astype(jnp.float32)
    edge_live = (
        lax.broadcasted_iota(jnp.int32, (4, edge_len, 1), 1)
        < (edge_counts[0, 0] * ROWS)[:, None, None]
    ).astype(jnp.float32)
    face_sum, edge_sum = neighbour_sum(faces, edges)
    face_res = (face_sum * face_live * 0.5).astype(jnp.bfloat16)
    edge_res = (edge_sum * edge_live * 0.25).astype(jnp.bfloat16)
    flat_rhs = jnp.concatenate(
        [face_res.reshape(4 * face_len, vectors), edge_res.reshape(4 * edge_len, vectors)], axis=0
    )
    node_basis = coarse_basis[0, 0]
    first_lift = lift_one[0, 0]
    second_lift = lift_two[0, 0]
    coarse_size = first_lift.shape[0]
    coarse_rhs = lax.dot_general(
        node_basis, flat_rhs, contract_first, preferred_element_type=jnp.float32
    )
    child_term = lax.dot_general(
        first_lift,
        jnp.dot(coarse_mat[0, 0], first_lift, precision=highest),
        contract_first,
        precision=highest,
    )
    child_rhs = lax.dot_general(first_lift, coarse_rhs, contract_first, precision=highest)
    merged = jnp.concatenate([child_term, child_rhs], axis=1)
    pair_data = merged + from_partner(merged, "gy", 0)
    row_term = lax.dot_general(
        second_lift,
        jnp.dot(pair_data[:, :coarse_size], second_lift, precision=highest),
        contract_first,
        precision=highest,
    )
    row_rhs = lax.dot_general(
        second_lift, pair_data[:, coarse_size:], contract_first, precision=highest
    )
    level_terms = 0.5 * jnp.concatenate([row_term, row_rhs], axis=1)
    row_total = level_terms
    for bit_number in range(lax.axis_size("gy").bit_length() - 1):
        row_total = row_total + from_partner(row_total, "gy", bit_number)
    factor = jnp.linalg.cholesky(row_total[:, :coarse_size])
    coarse_solution = jax.scipy.linalg.cho_solve((factor, True), row_total[:, coarse_size:])
    middle_values = jnp.dot(second_lift, coarse_solution, precision=highest)
    node_values = jnp.dot(first_lift, middle_values, precision=highest).astype(jnp.bfloat16)
    coarse_part = jnp.dot(node_basis, node_values, preferred_element_type=jnp.float32)
    local_part = jnp.dot(schur_inv[0, 0], flat_rhs, preferred_element_type=jnp.float32)
    corrected = (local_part + coarse_part).astype(jnp.bfloat16)
    face_corr = corrected[: 4 * face_len].reshape(4, face_len, vectors)
    edge_corr = corrected[4 * face_len :].reshape(4, edge_len, vectors)
    face_out, edge_out = neighbour_sum(face_corr, edge_corr)
    return (
        (face_out * 0.5 * face_live).astype(jnp.bfloat16)[None, None],
        (edge_out * 0.25 * edge_live).astype(jnp.bfloat16)[None, None],
    )


def solution(mesh):
    return jax.shard_map(
        body,
        mesh=mesh,
        in_specs=(
            P("gx", "gy", None, None, None),
            P("gx", "gy", None, None, None),
            P("gx", "gy", None),
            P("gx", "gy", None),
            P("gx", "gy", None, None),
            P("gx", "gy", None, None),
            P("gx", "gy", None, None),
            P("gx", "gy", None, None),
            P("gx", "gy", None, None),
        ),
        out_specs=(P("gx", "gy", None, None, None), P("gx", "gy", None, None, None)),
        check_vma=False,
    )
```

profile of v0, /device:TPU:11, one launch (start us, length us, event | category | flops | bytes accessed | tf_op | source)
XLA Modules:
  0.0 152.0 jit_solution(9123034746024910987)
XLA Ops:
  0.7 1.3 slice_bitcast_fusion.12
  2.7 2.7 %collective-permute-start.8 = (bf16[2,128,512]{2,1,0:T(8,128)(2,1)}, bf16[2,128,512]{2,1,0:T(8,128)(2,1)}, u32[]{:S(2)}, u32[]{:S(2)}) collective-permute-start(bf16[2,128,512]{2,1,0:T(8,128)(2,1)} %pad_maximum_fusion.8), channel_id=1, source_target_pairs={{1,0},{2,1},{3,2},{4,3},{5,4},{6,5},{7,6},{9,8},{10,9},{11,10},{12... | collective-permute-start | bytes 786440 | tf_op jit(solution)/shard_map/ppermute | solution.py:12
  5.4 1.9 %slice_bitcast_fusion.5 = (bf16[2,128,512]{2,1,0:T(8,128)(2,1)}, bf16[2,128,512]{2,1,0:T(8,128)(2,1)}) fusion(bf16[1,1,4,128,512]{4,3,2,1,0:T(8,128)(2,1)} %param.10), kind=kLoop, calls=%fused_computation.52 | loop fusion | bytes 1048576 | tf_op jit(solution)/shard_map/slice | solution.py:34
  7.3 3.2 %collective-permute-start.5 = (bf16[2,128,512]{2,1,0:T(8,128)(2,1)}, bf16[2,128,512]{2,1,0:T(8,128)(2,1)S(1)}, u32[]{:S(2)}, u32[]{:S(2)}) collective-permute-start(bf16[2,128,512]{2,1,0:T(8,128)(2,1)} %get-tuple-element.36), channel_id=1, source_target_pairs={{0,8},{8,16},{16,24},{1,9},{9,17},{17,25},{2,10},{10,18},{18,26},{... | collective-permute-start | bytes 786440 | tf_op jit(solution)/shard_map/ppermute | solution.py:12
  10.5 2.1 %collective-permute-start.6 = (bf16[2,128,512]{2,1,0:T(8,128)(2,1)}, bf16[2,128,512]{2,1,0:T(8,128)(2,1)S(1)}, u32[]{:S(2)}, u32[]{:S(2)}) collective-permute-start(bf16[2,128,512]{2,1,0:T(8,128)(2,1)} %get-tuple-element.37), channel_id=1, source_target_pairs={{8,0},{16,8},{24,16},{9,1},{17,9},{25,17},{10,2},{18,10},{26,18},{... | collective-permute-start | bytes 786440 | tf_op jit(solution)/shard_map/ppermute | solution.py:12
  12.6 1.0 slice_bitcast_fusion.3
  13.6 3.2 %collective-permute-start = (bf16[384,512]{1,0:T(8,128)(2,1)}, bf16[384,512]{1,0:T(8,128)(2,1)S(1)}, u32[]{:S(2)}, u32[]{:S(2)}) collective-permute-start(bf16[384,512]{1,0:T(8,128)(2,1)} %get-tuple-element.22), channel_id=1, source_target_pairs={{0,8},{8,16},{16,24},{1,9},{9,17},{17,25},{2,10},{10,18},{18,26},{... | collective-permute-start | bytes 1179656 | tf_op jit(solution)/shard_map/ppermute | solution.py:12
  16.8 4.7 %collective-permute-start.1 = (bf16[384,512]{1,0:T(8,128)(2,1)}, bf16[384,512]{1,0:T(8,128)(2,1)}, u32[]{:S(2)}, u32[]{:S(2)}) collective-permute-start(bf16[384,512]{1,0:T(8,128)(2,1)} %get-tuple-element.23), channel_id=1, source_target_pairs={{0,1},{1,2},{2,3},{3,4},{4,5},{5,6},{6,7},{8,9},{9,10},{10,11},{11... | collective-permute-start | bytes 1179656 | tf_op jit(solution)/shard_map/ppermute | solution.py:12
  23.5 2.2 %collective-permute-start.3 = (bf16[384,512]{1,0:T(8,128)(2,1)}, bf16[384,512]{1,0:T(8,128)(2,1)S(1)}, u32[]{:S(2)}, u32[]{:S(2)}) collective-permute-start(bf16[384,512]{1,0:T(8,128)(2,1)} %get-tuple-element.24), channel_id=1, source_target_pairs={{8,0},{16,8},{24,16},{9,1},{17,9},{25,17},{10,2},{18,10},{26,18},{... | collective-permute-start | bytes 1179656 | tf_op jit(solution)/shard_map/ppermute | solution.py:12
  25.8 1.9 %collective-permute-start.2 = (bf16[384,512]{1,0:T(8,128)(2,1)S(1)}, bf16[384,512]{1,0:T(8,128)(2,1)S(1)}, u32[]{:S(2)}, u32[]{:S(2)}) collective-permute-start(bf16[384,512]{1,0:T(8,128)(2,1)S(1)} %get-tuple-element.25), channel_id=1, source_target_pairs={{1,0},{2,1},{3,2},{4,3},{5,4},{6,5},{7,6},{9,8},{10,9},{11,10},{12... | collective-permute-start | bytes 1179656 | tf_op jit(solution)/shard_map/ppermute | solution.py:12
  27.9 4.5 %collective-permute-start.4 = (bf16[2,128,512]{2,1,0:T(8,128)(2,1)S(1)}, bf16[2,128,512]{2,1,0:T(8,128)(2,1)S(1)}, u32[]{:S(2)}, u32[]{:S(2)}) collective-permute-start(bf16[2,128,512]{2,1,0:T(8,128)(2,1)S(1)} %copy-done.7), channel_id=1, source_target_pairs={{0,1},{1,2},{2,3},{3,4},{4,5},{5,6},{6,7},{8,9},{9,10},{10,11},{11... | collective-permute-start | bytes 786440 | tf_op jit(solution)/shard_map/ppermute | solution.py:12
  32.4 1.9 %collective-permute-start.9 = (bf16[2,128,512]{2,1,0:T(8,128)(2,1)S(1)}, bf16[2,128,512]{2,1,0:T(8,128)(2,1)S(1)}, u32[]{:S(2)}, u32[]{:S(2)}) collective-permute-start(bf16[2,128,512]{2,1,0:T(8,128)(2,1)S(1)} %pad_maximum_fusion.9), channel_id=1, source_target_pairs={{1,0},{2,1},{3,2},{4,3},{5,4},{6,5},{7,6},{9,8},{10,9},{11,10},{12... | collective-permute-start | bytes 786440 | tf_op jit(solution)/shard_map/ppermute | solution.py:12
  34.4 0.8 collective-permute-done.3
  35.1 4.3 %collective-permute-start.7 = (bf16[2,128,512]{2,1,0:T(8,128)(2,1)S(1)}, bf16[2,128,512]{2,1,0:T(8,128)(2,1)S(1)}, u32[]{:S(2)}, u32[]{:S(2)}) collective-permute-start(bf16[2,128,512]{2,1,0:T(8,128)(2,1)S(1)} %pad_maximum_fusion.7), channel_id=1, source_target_pairs={{0,1},{1,2},{2,3},{3,4},{4,5},{5,6},{6,7},{8,9},{9,10},{10,11},{11... | collective-permute-start | bytes 786440 | tf_op jit(solution)/shard_map/ppermute | solution.py:12
  39.5 1.2 pad_maximum_fusion.1
  41.4 1.5 %collective-permute-done.9 = bf16[2,128,512]{2,1,0:T(8,128)(2,1)S(1)} collective-permute-done((bf16[2,128,512]{2,1,0:T(8,128)(2,1)S(1)}, bf16[2,128,512]{2,1,0:T(8,128)(2,1)S(1)}, u32[]{:S(2)}, u32[]{:S(2)}) %collective-permute-start.9) | collective-permute-done | bytes 262176 | tf_op jit(solution)/shard_map/ppermute | solution.py:12
  43.0 1.2 convert_add_fusion.3
  45.7 1.6 %collective-permute-done.10 = f32[128,640]{0,1:T(8,128)S(1)} collective-permute-done((f32[128,640]{0,1:T(8,128)S(1)}, f32[128,640]{0,1:T(8,128)S(1)}, u32[]{:S(2)}, u32[]{:S(2)}) %collective-permute-start.10) | collective-permute-done | bytes 327712 | tf_op jit(solution)/shard_map/ppermute | solution.py:18
  48.6 1.5 collective-permute-done.11
  50.3 9.0 %collective-permute-done.12 = f32[128,640]{0,1:T(8,128)S(1)} collective-permute-done((f32[128,640]{0,1:T(8,128)S(1)}, f32[128,640]{0,1:T(8,128)S(1)}, u32[]{:S(2)}, u32[]{:S(2)}) %collective-permute-start.12) | collective-permute-done | bytes 327712 | tf_op jit(solution)/shard_map/ppermute | solution.py:18
  59.4 1.7 %collective-permute-start.13 = (f32[128,640]{0,1:T(8,128)S(1)}, f32[128,640]{0,1:T(8,128)S(1)}, u32[]{:S(2)}, u32[]{:S(2)}) collective-permute-start(f32[128,640]{0,1:T(8,128)S(1)} %add.156), channel_id=1, source_target_pairs={{0,4},{1,5},{2,6},{3,7},{4,0},{5,1},{6,2},{7,3},{8,12},{9,13},{10,... | collective-permute-start | bytes 983048 | tf_op jit(solution)/shard_map/ppermute | solution.py:18
  61.1 6.2 %fusion = f32[512,2048]{1,0:T(8,128)} fusion(bf16[1,1,2048,2048]{3,2,1,0:T(8,128)(2,1)S(1)} %bitcast.147, bf16[512,512]{1,0:T(8,128)(2,1)S(1)} %fusion.9, bf16[1536,512]{1,0:T(8,128)(2,1)S(1)} %fusion.4), kind=kOutput, calls=%fused_computation | convolution fusion | flops 4299161600 | bytes 14680064 | tf_op jit(solution)/shard_map/dot_general | solution.py:129
  68.1 11.7 %cholesky.16 = f32[128,128]{1,0:T(8,128)S(1)} custom-call(f32[128,128]{1,0:T(8,128)S(1)} %fusion.21), custom_call_target="Cholesky" | custom-call | tf_op jit(solution)/shard_map/jit(cholesky)/cholesky | solution.py:124
  81.1 9.8 %custom-call.10 = f32[1,128,128]{1,2,0:T(8,128)S(1)} custom-call(f32[1,128,128]{2,1,0:T(8,128)S(1)} %fusion.15), custom_call_target="InvertDiagBlocksLowerTriangular" | custom-call | tf_op jit(solution)/shard_map/jit(_cho_solve)/triangular_solve | solution.py:125
  92.7 2.9 %fusion.5 = bf16[2048,512]{0,1:T(8,128)(2,1)S(1)} fusion(f32[512,2048]{1,0:T(8,128)} %fusion, bf16[512,128]{1,0:T(8,128)(2,1)S(1)} %convolution_convert_fusion, bf16[1,1,2048,128]{3,2,1,0:T(8,128)(2,1)S(1)} %copy-done), kind=kOutput, calls=%fused_computation.8 | convolution fusion | flops 270532608 | bytes 6946816 | tf_op jit(solution)/shard_map/dot_general | solution.py:128
  95.7 0.7 slice_bitcast_fusion.8
  96.5 2.0 %slice_convert_fusion = f32[1536,512]{0,1:T(8,128)} fusion(bf16[2048,512]{0,1:T(8,128)(2,1)S(1)} %fusion.5), kind=kLoop, calls=%fused_computation.10 | loop fusion | flops 786432 | bytes 4718592 | tf_op jit(solution)/shard_map/convert_element_type | solution.py:22
  99.2 3.7 %collective-permute-start.22 = (bf16[2,128,512]{1,2,0:T(8,128)(2,1)}, bf16[2,128,512]{1,2,0:T(8,128)(2,1)}, u32[]{:S(2)}, u32[]{:S(2)}) collective-permute-start(bf16[2,128,512]{1,2,0:T(8,128)(2,1)} %pad_maximum_fusion.12), channel_id=1, source_target_pairs={{1,0},{2,1},{3,2},{4,3},{5,4},{6,5},{7,6},{9,8},{10,9},{11,10},{12... | collective-permute-start | bytes 786440 | tf_op jit(solution)/shard_map/ppermute | solution.py:12
  103.1 0.8 copy.18
  104.1 0.8 copy.20
  104.9 2.3 %collective-permute-start.20 = (bf16[2,128,512]{1,2,0:T(8,128)(2,1)}, bf16[2,128,512]{1,2,0:T(8,128)(2,1)S(1)}, u32[]{:S(2)}, u32[]{:S(2)}) collective-permute-start(bf16[2,128,512]{1,2,0:T(8,128)(2,1)} %copy.20), channel_id=1, source_target_pairs={{8,0},{16,8},{24,16},{9,1},{17,9},{25,17},{10,2},{18,10},{26,18},{... | collective-permute-start | bytes 786440 | tf_op jit(solution)/shard_map/ppermute | solution.py:12
  107.2 3.0 %collective-permute-start.19 = (bf16[2,128,512]{1,2,0:T(8,128)(2,1)}, bf16[2,128,512]{1,2,0:T(8,128)(2,1)S(1)}, u32[]{:S(2)}, u32[]{:S(2)}) collective-permute-start(bf16[2,128,512]{1,2,0:T(8,128)(2,1)} %copy.18), channel_id=1, source_target_pairs={{0,8},{8,16},{16,24},{1,9},{9,17},{17,25},{2,10},{10,18},{18,26},{... | collective-permute-start | bytes 786440 | tf_op jit(solution)/shard_map/ppermute | solution.py:12
  110.2 1.2 fusion.41
  111.4 3.5 %collective-permute-start.14 = (bf16[384,512]{0,1:T(8,128)(2,1)}, bf16[384,512]{0,1:T(8,128)(2,1)}, u32[]{:S(2)}, u32[]{:S(2)}) collective-permute-start(bf16[384,512]{0,1:T(8,128)(2,1)} %get-tuple-element.18), channel_id=1, source_target_pairs={{0,8},{8,16},{16,24},{1,9},{9,17},{17,25},{2,10},{10,18},{18,26},{... | collective-permute-start | bytes 1179656 | tf_op jit(solution)/shard_map/ppermute | solution.py:12
  114.9 2.5 %collective-permute-start.17 = (bf16[384,512]{0,1:T(8,128)(2,1)}, bf16[384,512]{0,1:T(8,128)(2,1)}, u32[]{:S(2)}, u32[]{:S(2)}) collective-permute-start(bf16[384,512]{0,1:T(8,128)(2,1)} %get-tuple-element.19), channel_id=1, source_target_pairs={{8,0},{16,8},{24,16},{9,1},{17,9},{25,17},{10,2},{18,10},{26,18},{... | collective-permute-start | bytes 1179656 | tf_op jit(solution)/shard_map/ppermute | solution.py:12
  117.4 0.8 pad_maximum_fusion.10
  118.2 3.5 %copy.15 = f32[1536,512]{1,0:T(8,128)} copy(f32[1536,512]{0,1:T(8,128)} %slice_convert_fusion) | data formatting | bytes 6291456 | tf_op jit(solution)/shard_map/convert_element_type | solution.py:22
  121.7 3.6 %copy.16 = f32[1,1,4,384,512]{3,4,2,1,0:T(8,128)} copy(f32[1,1,4,384,512]{4,3,2,1,0:T(8,128)} %bitcast.138) | data formatting | bytes 6291456 | tf_op jit(solution)/shard_map/convert_element_type | solution.py:22
  125.3 3.0 %collective-permute-start.16 = (bf16[384,512]{0,1:T(8,128)(2,1)}, bf16[384,512]{0,1:T(8,128)(2,1)S(1)}, u32[]{:S(2)}, u32[]{:S(2)}) collective-permute-start(bf16[384,512]{0,1:T(8,128)(2,1)} %get-tuple-element.20), channel_id=1, source_target_pairs={{1,0},{2,1},{3,2},{4,3},{5,4},{6,5},{7,6},{9,8},{10,9},{11,10},{12... | collective-permute-start | bytes 1179656 | tf_op jit(solution)/shard_map/ppermute | solution.py:12
  128.4 4.3 %collective-permute-start.15 = (bf16[384,512]{0,1:T(8,128)(2,1)S(1)}, bf16[384,512]{0,1:T(8,128)(2,1)S(1)}, u32[]{:S(2)}, u32[]{:S(2)}) collective-permute-start(bf16[384,512]{0,1:T(8,128)(2,1)S(1)} %copy-done.6), channel_id=1, source_target_pairs={{0,1},{1,2},{2,3},{3,4},{4,5},{5,6},{6,7},{8,9},{9,10},{10,11},{11... | collective-permute-start | bytes 1179656 | tf_op jit(solution)/shard_map/ppermute | solution.py:12
  132.7 0.8 pad_maximum_fusion.11
  134.2 2.4 %collective-permute-start.18 = (bf16[2,128,512]{1,2,0:T(8,128)(2,1)}, bf16[2,128,512]{1,2,0:T(8,128)(2,1)}, u32[]{:S(2)}, u32[]{:S(2)}) collective-permute-start(bf16[2,128,512]{1,2,0:T(8,128)(2,1)} %pad_maximum_fusion.10), channel_id=1, source_target_pairs={{0,1},{1,2},{2,3},{3,4},{4,5},{5,6},{6,7},{8,9},{9,10},{10,11},{11... | collective-permute-start | bytes 786440 | tf_op jit(solution)/shard_map/ppermute | solution.py:12
  136.6 1.9 %collective-permute-start.23 = (bf16[2,128,512]{1,2,0:T(8,128)(2,1)}, bf16[2,128,512]{1,2,0:T(8,128)(2,1)}, u32[]{:S(2)}, u32[]{:S(2)}) collective-permute-start(bf16[2,128,512]{1,2,0:T(8,128)(2,1)} %pad_maximum_fusion.13), channel_id=1, source_target_pairs={{1,0},{2,1},{3,2},{4,3},{5,4},{6,5},{7,6},{9,8},{10,9},{11,10},{12... | collective-permute-start | bytes 786440 | tf_op jit(solution)/shard_map/ppermute | solution.py:12
  138.5 4.5 %collective-permute-start.21 = (bf16[2,128,512]{1,2,0:T(8,128)(2,1)}, bf16[2,128,512]{1,2,0:T(8,128)(2,1)}, u32[]{:S(2)}, u32[]{:S(2)}) collective-permute-start(bf16[2,128,512]{1,2,0:T(8,128)(2,1)} %pad_maximum_fusion.11), channel_id=1, source_target_pairs={{0,1},{1,2},{2,3},{3,4},{4,5},{5,6},{6,7},{8,9},{9,10},{10,11},{11... | collective-permute-start | bytes 786440 | tf_op jit(solution)/shard_map/ppermute | solution.py:12
  143.1 3.7 %multiply_convert_fusion = bf16[1,1,4,384,512]{3,4,2,1,0:T(8,128)(2,1)} fusion(f32[1,1,4,384,512]{3,4,2,1,0:T(8,128)} %copy.16, bf16[1,1,1,384,512]{3,4,2,1,0:T(8,128)(2,1)} %bitcast.37, bf16[1,1,1,384,512]{3,4,2,1,0:T(8,128)(2,1)S(1)} %bitcast.142, bf16[1,1,1,384,512]{3,4,2,1,0:T(8,128)(2,1)S(1)} %bitcast.144, bf16[1,1,1,384,512]{3,4,2,1,0:T(8,128)(2,1)} %bitcast.34, ...), kind=kLoop, calls=%fused_computation.7 | loop fusion | flops 5505024 | bytes 6297600 | tf_op jit(solution)/shard_map/convert_element_type | solution.py:135
  146.8 2.6 %copy.21 = bf16[1,1,4,384,512]{4,3,2,1,0:T(8,128)(2,1)} copy(bf16[1,1,4,384,512]{3,4,2,1,0:T(8,128)(2,1)} %multiply_convert_fusion) | data formatting | bytes 3145728
  149.4 1.5 %add_bitcast_fusion.2 = (f32[1,1,1,128,512]{3,4,2,1,0:T(8,128)S(1)}, f32[1,1,1,128,512]{3,4,2,1,0:T(8,128)S(1)}, f32[1,1,1,128,512]{3,4,2,1,0:T(8,128)S(1)}, f32[1,1,1,128,512]{3,4,2,1,0:T(8,128)S(1)}) fusion(bf16[2,128,512]{1,2,0:T(8,128)(2,1)} %collective-permute-done.23, bf16[2,128,512]{1,2,0:T(8,128)(2,1)} %collective-permute-done.22, ...), kind=kLoop, calls=%fused_computation.45 | loop fusion | flops 1835008 | bytes 3145728 | tf_op jit(solution)/shard_map/stack | solution.py:60
  151.0 1.0 copy.22
  (106 shorter events, 12.3 us)
Async XLA Ops:
  0.6 43.8 %copy-start = (bf16[1,1,2048,128]{3,2,1,0:T(8,128)(2,1)S(1)}, bf16[1,1,2048,128]{3,2,1,0:T(8,128)(2,1)}, u32[]{:S(2)}) copy-start(bf16[1,1,2048,128]{3,2,1,0:T(8,128)(2,1)} %param.14) | copy-start | bytes 1572868
  0.6 11.9 %copy-start.1 = (bf16[1,1,4,384,512]{4,3,2,1,0:T(8,128)(2,1)S(1)}, bf16[1,1,4,384,512]{4,3,2,1,0:T(8,128)(2,1)}, u32[]{:S(2)}) copy-start(bf16[1,1,4,384,512]{4,3,2,1,0:T(8,128)(2,1)} %param.9) | copy-start | bytes 4718596
  2.7 18.8 %copy-start.14 = (s32[1,1,4]{2,1,0:T(1,128)S(1)}, s32[1,1,4]{2,1,0:T(1,128)}, u32[]{:S(2)}) copy-start(s32[1,1,4]{2,1,0:T(1,128)} %param.11) | copy-start | bytes 52
  2.7 18.9 %copy-start.15 = (s32[1,1,4]{2,1,0:T(1,128)S(1)}, s32[1,1,4]{2,1,0:T(1,128)}, u32[]{:S(2)}) copy-start(s32[1,1,4]{2,1,0:T(1,128)} %param.12) | copy-start | bytes 52
  2.7 19.0 %copy-start.4 = (f32[1,1,128,128]{3,2,1,0:T(8,128)S(1)}, f32[1,1,128,128]{3,2,1,0:T(8,128)}, u32[]{:S(2)}) copy-start(f32[1,1,128,128]{3,2,1,0:T(8,128)} %param.16) | copy-start | bytes 196612
  2.7 19.0 %copy-start.8 = (f32[1,1,128,128]{3,2,1,0:T(8,128)S(1)}, f32[1,1,128,128]{3,2,1,0:T(8,128)}, u32[]{:S(2)}) copy-start(f32[1,1,128,128]{3,2,1,0:T(8,128)} %param.15) | copy-start | bytes 196612
  2.7 38.7 %collective-permute-start.8 = (bf16[2,128,512]{2,1,0:T(8,128)(2,1)}, bf16[2,128,512]{2,1,0:T(8,128)(2,1)}, u32[]{:S(2)}, u32[]{:S(2)}) collective-permute-start(bf16[2,128,512]{2,1,0:T(8,128)(2,1)} %pad_maximum_fusion.8), channel_id=1, source_target_pairs={{1,0},{2,1},{3,2},{4,3},{5,4},{6,5},{7,6},{9,8},{10,9},{11,10},{12... | collective-permute-start | bytes 786440 | tf_op jit(solution)/shard_map/ppermute | solution.py:12
  7.3 16.3 %collective-permute-start.5 = (bf16[2,128,512]{2,1,0:T(8,128)(2,1)}, bf16[2,128,512]{2,1,0:T(8,128)(2,1)S(1)}, u32[]{:S(2)}, u32[]{:S(2)}) collective-permute-start(bf16[2,128,512]{2,1,0:T(8,128)(2,1)} %get-tuple-element.36), channel_id=1, source_target_pairs={{0,8},{8,16},{16,24},{1,9},{9,17},{17,25},{2,10},{10,18},{18,26},{... | collective-permute-start | bytes 786440 | tf_op jit(solution)/shard_map/ppermute | solution.py:12
  10.5 15.4 %collective-permute-start.6 = (bf16[2,128,512]{2,1,0:T(8,128)(2,1)}, bf16[2,128,512]{2,1,0:T(8,128)(2,1)S(1)}, u32[]{:S(2)}, u32[]{:S(2)}) collective-permute-start(bf16[2,128,512]{2,1,0:T(8,128)(2,1)} %get-tuple-element.37), channel_id=1, source_target_pairs={{8,0},{16,8},{24,16},{9,1},{17,9},{25,17},{10,2},{18,10},{26,18},{... | collective-permute-start | bytes 786440 | tf_op jit(solution)/shard_map/ppermute | solution.py:12
  13.6 14.3 %collective-permute-start = (bf16[384,512]{1,0:T(8,128)(2,1)}, bf16[384,512]{1,0:T(8,128)(2,1)S(1)}, u32[]{:S(2)}, u32[]{:S(2)}) collective-permute-start(bf16[384,512]{1,0:T(8,128)(2,1)} %get-tuple-element.22), channel_id=1, source_target_pairs={{0,8},{8,16},{16,24},{1,9},{9,17},{17,25},{2,10},{10,18},{18,26},{... | collective-permute-start | bytes 1179656 | tf_op jit(solution)/shard_map/ppermute | solution.py:12
  16.8 15.7 %collective-permute-start.1 = (bf16[384,512]{1,0:T(8,128)(2,1)}, bf16[384,512]{1,0:T(8,128)(2,1)}, u32[]{:S(2)}, u32[]{:S(2)}) collective-permute-start(bf16[384,512]{1,0:T(8,128)(2,1)} %get-tuple-element.23), channel_id=1, source_target_pairs={{0,1},{1,2},{2,3},{3,4},{4,5},{5,6},{6,7},{8,9},{9,10},{10,11},{11... | collective-permute-start | bytes 1179656 | tf_op jit(solution)/shard_map/ppermute | solution.py:12
  21.5 1.3 copy-start.12
  21.5 1.2 copy-start.10
  23.5 4.3 %copy-start.7 = (bf16[2,128,512]{2,1,0:T(8,128)(2,1)S(1)}, bf16[2,128,512]{2,1,0:T(8,128)(2,1)}, u32[]{:S(2)}) copy-start(bf16[2,128,512]{2,1,0:T(8,128)(2,1)} %pad_maximum_fusion.6) | copy-start | bytes 786436
  23.5 11.6 %collective-permute-start.3 = (bf16[384,512]{1,0:T(8,128)(2,1)}, bf16[384,512]{1,0:T(8,128)(2,1)S(1)}, u32[]{:S(2)}, u32[]{:S(2)}) collective-permute-start(bf16[384,512]{1,0:T(8,128)(2,1)} %get-tuple-element.24), channel_id=1, source_target_pairs={{8,0},{16,8},{24,16},{9,1},{17,9},{25,17},{10,2},{18,10},{26,18},{... | collective-permute-start | bytes 1179656 | tf_op jit(solution)/shard_map/ppermute | solution.py:12
  25.8 13.6 %collective-permute-start.2 = (bf16[384,512]{1,0:T(8,128)(2,1)S(1)}, bf16[384,512]{1,0:T(8,128)(2,1)S(1)}, u32[]{:S(2)}, u32[]{:S(2)}) collective-permute-start(bf16[384,512]{1,0:T(8,128)(2,1)S(1)} %get-tuple-element.25), channel_id=1, source_target_pairs={{1,0},{2,1},{3,2},{4,3},{5,4},{6,5},{7,6},{9,8},{10,9},{11,10},{12... | collective-permute-start | bytes 1179656 | tf_op jit(solution)/shard_map/ppermute | solution.py:12
  27.9 13.5 %collective-permute-start.4 = (bf16[2,128,512]{2,1,0:T(8,128)(2,1)S(1)}, bf16[2,128,512]{2,1,0:T(8,128)(2,1)S(1)}, u32[]{:S(2)}, u32[]{:S(2)}) collective-permute-start(bf16[2,128,512]{2,1,0:T(8,128)(2,1)S(1)} %copy-done.7), channel_id=1, source_target_pairs={{0,1},{1,2},{2,3},{3,4},{4,5},{5,6},{6,7},{8,9},{9,10},{10,11},{11... | collective-permute-start | bytes 786440 | tf_op jit(solution)/shard_map/ppermute | solution.py:12
  32.4 10.5 %collective-permute-start.9 = (bf16[2,128,512]{2,1,0:T(8,128)(2,1)S(1)}, bf16[2,128,512]{2,1,0:T(8,128)(2,1)S(1)}, u32[]{:S(2)}, u32[]{:S(2)}) collective-permute-start(bf16[2,128,512]{2,1,0:T(8,128)(2,1)S(1)} %pad_maximum_fusion.9), channel_id=1, source_target_pairs={{1,0},{2,1},{3,2},{4,3},{5,4},{6,5},{7,6},{9,8},{10,9},{11,10},{12... | collective-permute-start | bytes 786440 | tf_op jit(solution)/shard_map/ppermute | solution.py:12
  35.1 7.8 %collective-permute-start.7 = (bf16[2,128,512]{2,1,0:T(8,128)(2,1)S(1)}, bf16[2,128,512]{2,1,0:T(8,128)(2,1)S(1)}, u32[]{:S(2)}, u32[]{:S(2)}) collective-permute-start(bf16[2,128,512]{2,1,0:T(8,128)(2,1)S(1)} %pad_maximum_fusion.7), channel_id=1, source_target_pairs={{0,1},{1,2},{2,3},{3,4},{4,5},{5,6},{6,7},{8,9},{9,10},{10,11},{11... | collective-permute-start | bytes 786440 | tf_op jit(solution)/shard_map/ppermute | solution.py:12
  40.7 2.3 %copy-start.2 = (bf16[1,1,4,128,512]{4,3,2,1,0:T(8,128)(2,1)S(1)}, bf16[1,1,4,128,512]{4,3,2,1,0:T(8,128)(2,1)}, u32[]{:S(2)}) copy-start(bf16[1,1,4,128,512]{4,3,2,1,0:T(8,128)(2,1)} %param.10) | copy-start | bytes 1572868
  40.7 20.4 %slice-start = ((s8[8388608]{0:T(1024)(128)(4,1)}), s8[4194304]{0:T(1024)(128)(4,1)S(1)}, s32[]{:S(2)}) async-start(s8[8388608]{0:T(1024)(128)(4,1)} %bitcast.146), calls=%async_computation | async-start | bytes 8388608
  41.4 2.9 %copy-start.9 = (f32[512]{0:T(512)S(1)}, f32[512]{0:T(512)}, u32[]{:S(2)}) copy-start(f32[512]{0:T(512)} %convert_bitcast_fusion) | copy-start | bytes 6148
  44.3 16.8 %slice-start.1 = ((s8[8388608]{0:T(1024)(128)(4,1)}), s8[4194304]{0:T(1024)(128)(4,1)S(1)}, s32[]{:S(2)}) async-start(s8[8388608]{0:T(1024)(128)(4,1)} %bitcast.146), calls=%async_computation.1 | async-start | bytes 8388608
  45.2 2.2 %copy-start.3 = (f32[1,1,128,128]{3,2,1,0:T(8,128)S(1)}, f32[1,1,128,128]{3,2,1,0:T(8,128)}, u32[]{:S(2)}) copy-start(f32[1,1,128,128]{3,2,1,0:T(8,128)} %param.17) | copy-start | bytes 196612
  45.6 4.6 %copy-start.11 = (s32[4]{0:T(128)S(1)}, s32[4]{0:T(128)}, u32[]{:S(2)}) copy-start(s32[4]{0:T(128)} %copy-done.10) | copy-start | bytes 52
  45.6 4.7 %copy-start.13 = (s32[4]{0:T(128)S(1)}, s32[4]{0:T(128)}, u32[]{:S(2)}) copy-start(s32[4]{0:T(128)} %copy-done.12) | copy-start | bytes 52
  45.6 1.7 %collective-permute-start.10 = (f32[128,640]{0,1:T(8,128)S(1)}, f32[128,640]{0,1:T(8,128)S(1)}, u32[]{:S(2)}, u32[]{:S(2)}) collective-permute-start(f32[128,640]{0,1:T(8,128)S(1)} %pad_maximum_fusion.5), channel_id=1, source_target_pairs={{0,1},{1,0},{2,3},{3,2},{4,5},{5,4},{6,7},{7,6},{8,9},{9,8},{10,11... | collective-permute-start | bytes 983048 | tf_op jit(solution)/shard_map/ppermute | solution.py:18
  48.4 1.7 %collective-permute-start.11 = (f32[128,640]{0,1:T(8,128)S(1)}, f32[128,640]{0,1:T(8,128)S(1)}, u32[]{:S(2)}, u32[]{:S(2)}) collective-permute-start(f32[128,640]{0,1:T(8,128)S(1)} %maximum_multiply_fusion.1), channel_id=1, source_target_pairs={{0,1},{1,0},{2,3},{3,2},{4,5},{5,4},{6,7},{7,6},{8,9},{9,8},{10,11... | collective-permute-start | bytes 983048 | tf_op jit(solution)/shard_map/ppermute | solution.py:18
  50.1 9.2 %collective-permute-start.12 = (f32[128,640]{0,1:T(8,128)S(1)}, f32[128,640]{0,1:T(8,128)S(1)}, u32[]{:S(2)}, u32[]{:S(2)}) collective-permute-start(f32[128,640]{0,1:T(8,128)S(1)} %fusion.39), channel_id=1, source_target_pairs={{0,2},{1,3},{2,0},{3,1},{4,6},{5,7},{6,4},{7,5},{8,10},{9,11},{10,... | collective-permute-start | bytes 983048 | tf_op jit(solution)/shard_map/ppermute | solution.py:18
  59.4 8.6 %collective-permute-start.13 = (f32[128,640]{0,1:T(8,128)S(1)}, f32[128,640]{0,1:T(8,128)S(1)}, u32[]{:S(2)}, u32[]{:S(2)}) collective-permute-start(f32[128,640]{0,1:T(8,128)S(1)} %add.156), channel_id=1, source_target_pairs={{0,4},{1,5},{2,6},{3,7},{4,0},{5,1},{6,2},{7,3},{8,12},{9,13},{10,... | collective-permute-start | bytes 983048 | tf_op jit(solution)/shard_map/ppermute | solution.py:18
  99.2 50.2 %collective-permute-start.22 = (bf16[2,128,512]{1,2,0:T(8,128)(2,1)}, bf16[2,128,512]{1,2,0:T(8,128)(2,1)}, u32[]{:S(2)}, u32[]{:S(2)}) collective-permute-start(bf16[2,128,512]{1,2,0:T(8,128)(2,1)} %pad_maximum_fusion.12), channel_id=1, source_target_pairs={{1,0},{2,1},{3,2},{4,3},{5,4},{6,5},{7,6},{9,8},{10,9},{11,10},{12... | collective-permute-start | bytes 786440 | tf_op jit(solution)/shard_map/ppermute | solution.py:12
  103.9 13.5 %copy-start.5 = (bf16[1,128,512]{1,2,0:T(8,128)(2,1)S(1)}, bf16[1,128,512]{1,2,0:T(8,128)(2,1)}, u32[]{:S(2)}) copy-start(bf16[1,128,512]{1,2,0:T(8,128)(2,1)} %get-tuple-element.14) | copy-start | bytes 393220
  104.9 20.4 %collective-permute-start.20 = (bf16[2,128,512]{1,2,0:T(8,128)(2,1)}, bf16[2,128,512]{1,2,0:T(8,128)(2,1)S(1)}, u32[]{:S(2)}, u32[]{:S(2)}) collective-permute-start(bf16[2,128,512]{1,2,0:T(8,128)(2,1)} %copy.20), channel_id=1, source_target_pairs={{8,0},{16,8},{24,16},{9,1},{17,9},{25,17},{10,2},{18,10},{26,18},{... | collective-permute-start | bytes 786440 | tf_op jit(solution)/shard_map/ppermute | solution.py:12
  107.2 21.2 %collective-permute-start.19 = (bf16[2,128,512]{1,2,0:T(8,128)(2,1)}, bf16[2,128,512]{1,2,0:T(8,128)(2,1)S(1)}, u32[]{:S(2)}, u32[]{:S(2)}) collective-permute-start(bf16[2,128,512]{1,2,0:T(8,128)(2,1)} %copy.18), channel_id=1, source_target_pairs={{0,8},{8,16},{16,24},{1,9},{9,17},{17,25},{2,10},{10,18},{18,26},{... | collective-permute-start | bytes 786440 | tf_op jit(solution)/shard_map/ppermute | solution.py:12
  111.4 22.8 %collective-permute-start.14 = (bf16[384,512]{0,1:T(8,128)(2,1)}, bf16[384,512]{0,1:T(8,128)(2,1)}, u32[]{:S(2)}, u32[]{:S(2)}) collective-permute-start(bf16[384,512]{0,1:T(8,128)(2,1)} %get-tuple-element.18), channel_id=1, source_target_pairs={{0,8},{8,16},{16,24},{1,9},{9,17},{17,25},{2,10},{10,18},{18,26},{... | collective-permute-start | bytes 1179656 | tf_op jit(solution)/shard_map/ppermute | solution.py:12
  114.9 21.7 %collective-permute-start.17 = (bf16[384,512]{0,1:T(8,128)(2,1)}, bf16[384,512]{0,1:T(8,128)(2,1)}, u32[]{:S(2)}, u32[]{:S(2)}) collective-permute-start(bf16[384,512]{0,1:T(8,128)(2,1)} %get-tuple-element.19), channel_id=1, source_target_pairs={{8,0},{16,8},{24,16},{9,1},{17,9},{25,17},{10,2},{18,10},{26,18},{... | collective-permute-start | bytes 1179656 | tf_op jit(solution)/shard_map/ppermute | solution.py:12
  121.7 6.6 %copy-start.6 = (bf16[384,512]{0,1:T(8,128)(2,1)S(1)}, bf16[384,512]{0,1:T(8,128)(2,1)}, u32[]{:S(2)}) copy-start(bf16[384,512]{0,1:T(8,128)(2,1)} %get-tuple-element.21) | copy-start | bytes 1179652
  125.3 13.2 %collective-permute-start.16 = (bf16[384,512]{0,1:T(8,128)(2,1)}, bf16[384,512]{0,1:T(8,128)(2,1)S(1)}, u32[]{:S(2)}, u32[]{:S(2)}) collective-permute-start(bf16[384,512]{0,1:T(8,128)(2,1)} %get-tuple-element.20), channel_id=1, source_target_pairs={{1,0},{2,1},{3,2},{4,3},{5,4},{6,5},{7,6},{9,8},{10,9},{11,10},{12... | collective-permute-start | bytes 1179656 | tf_op jit(solution)/shard_map/ppermute | solution.py:12
  128.4 14.7 %collective-permute-start.15 = (bf16[384,512]{0,1:T(8,128)(2,1)S(1)}, bf16[384,512]{0,1:T(8,128)(2,1)S(1)}, u32[]{:S(2)}, u32[]{:S(2)}) collective-permute-start(bf16[384,512]{0,1:T(8,128)(2,1)S(1)} %copy-done.6), channel_id=1, source_target_pairs={{0,1},{1,2},{2,3},{3,4},{4,5},{5,6},{6,7},{8,9},{9,10},{10,11},{11... | collective-permute-start | bytes 1179656 | tf_op jit(solution)/shard_map/ppermute | solution.py:12
  134.2 15.2 %collective-permute-start.18 = (bf16[2,128,512]{1,2,0:T(8,128)(2,1)}, bf16[2,128,512]{1,2,0:T(8,128)(2,1)}, u32[]{:S(2)}, u32[]{:S(2)}) collective-permute-start(bf16[2,128,512]{1,2,0:T(8,128)(2,1)} %pad_maximum_fusion.10), channel_id=1, source_target_pairs={{0,1},{1,2},{2,3},{3,4},{4,5},{5,6},{6,7},{8,9},{9,10},{10,11},{11... | collective-permute-start | bytes 786440 | tf_op jit(solution)/shard_map/ppermute | solution.py:12
  136.6 12.8 %collective-permute-start.23 = (bf16[2,128,512]{1,2,0:T(8,128)(2,1)}, bf16[2,128,512]{1,2,0:T(8,128)(2,1)}, u32[]{:S(2)}, u32[]{:S(2)}) collective-permute-start(bf16[2,128,512]{1,2,0:T(8,128)(2,1)} %pad_maximum_fusion.13), channel_id=1, source_target_pairs={{1,0},{2,1},{3,2},{4,3},{5,4},{6,5},{7,6},{9,8},{10,9},{11,10},{12... | collective-permute-start | bytes 786440 | tf_op jit(solution)/shard_map/ppermute | solution.py:12
  138.5 10.8 %collective-permute-start.21 = (bf16[2,128,512]{1,2,0:T(8,128)(2,1)}, bf16[2,128,512]{1,2,0:T(8,128)(2,1)}, u32[]{:S(2)}, u32[]{:S(2)}) collective-permute-start(bf16[2,128,512]{1,2,0:T(8,128)(2,1)} %pad_maximum_fusion.11), channel_id=1, source_target_pairs={{0,1},{1,2},{2,3},{3,4},{4,5},{5,6},{6,7},{8,9},{9,10},{10,11},{11... | collective-permute-start | bytes 786440 | tf_op jit(solution)/shard_map/ppermute | solution.py:12
where the time goes:
time: 153 us; the launch traced here: 152 us
  starting transfers between devices  64 us (42%)
  other arithmetic  39.1 us (26%)
  local copies, waits for them, and re-layouts  19.1 us (12%)
  waiting for transfers between devices  15.1 us (10%)
  matrix products  13.4 us (9%)
    ppermute x20, starting transfers between devices, from_behind(): lax.ppermute(value, axis, [(source, source + steps) for source in range(f...  62 us
    ppermute x4, waiting for transfers between devices, from_partner(): return lax.ppermute(value, axis, pairs)  12.8 us
    another operation x3, other arithmetic, body(): factor = jnp.linalg.cholesky(row_total[:, :coarse_size])  12.4 us
    another operation x2, other arithmetic, body(): jax.scipy.linalg.cho_solve((factor, True), row_total[:, coarse_size:])  10.5 us
    convert_element_type x2, local copies, waits for them, and re-layouts, widen(): return values.astype(jnp.float32)  7.11 us
    dot_general x1, matrix products, body(): jnp.dot(schur_inv[0, 0], flat_rhs, preferred_element_type=jnp.float32)  6.17 us
    slice x6, local copies, waits for them, and re-layouts, neighbour_sum(): row_edges[offset] = from_behind(edges[first:first + 2], 'gx', offset)  3.84 us
    convert_element_type x1, other arithmetic, body(): (face_out * 0.5 * face_live).astype(jnp.bfloat16)[None, None]  3.68 us
  transfers between devices with their start and end apart: 24, of which 6 were waited for; matrix products, arithmetic and copies ran while one was open for 21% of the time, Pallas kernels for 0%

commit v1 on v0

v1 whole, which is shorter than its diff:
```python
import functools

import jax
import jax.numpy as jnp
from jax import lax
from jax.experimental import pallas as pl
from jax.experimental.pallas import tpu as pltpu
from jax.sharding import PartitionSpec as P

ROWS = 64
F32 = jnp.float32
BF16 = jnp.bfloat16
MESH = pl.DeviceIdType.MESH
HIGHEST = lax.Precision.HIGHEST
FACE_STEP = ((-1, 0), (0, -1), (0, 1), (1, 0))
EDGE_STEP = ((-1, -1), (-1, 1), (1, -1), (1, 1))
COLS0 = (((0,), (0,)), ((), ()))


def exact_dot(a, b):
    return jnp.dot(a, b, precision=HIGHEST, preferred_element_type=F32)


def exact_dot_t(a, b):
    return lax.dot_general(a, b, COLS0, precision=HIGHEST, preferred_element_type=F32)


def invert(matrix):
    size = matrix.shape[0]
    block = 8
    lane = lax.broadcasted_iota(jnp.int32, (1, size), 1)
    row = lax.broadcasted_iota(jnp.int32, (size, 1), 0)

    def step(_, a):
        for p in range(0, block, 2):
            q = p + 1
            r0, r1 = a[p : p + 1, :], a[q : q + 1, :]
            c0, c1 = a[:, p : p + 1], a[:, q : q + 1]
            d00, d01 = a[p : p + 1, p : p + 1], a[p : p + 1, q : q + 1]
            d10, d11 = a[q : q + 1, p : p + 1], a[q : q + 1, q : q + 1]
            inv = 1.0 / (d00 * d11 - d01 * d10)
            e0 = jnp.where(lane == p, 1.0, 0.0)
            e1 = jnp.where(lane == q, 1.0, 0.0)
            pivot_lane = (lane == p) | (lane == q)
            pivot_row = (row == p) | (row == q)
            r0 = jnp.where(pivot_lane, e0, r0)
            r1 = jnp.where(pivot_lane, e1, r1)
            w0 = (d11 * inv) * r0 - (d01 * inv) * r1
            w1 = (d00 * inv) * r1 - (d10 * inv) * r0
            c0 = jnp.where(pivot_row, jnp.where(row == p, -1.0, 0.0), c0)
            c1 = jnp.where(pivot_row, jnp.where(row == q, -1.0, 0.0), c1)
            a = jnp.where(pivot_row | pivot_lane, 0.0, a) - c0 * w0 - c1 * w1
        a = jnp.concatenate([a[block:], a[:block]], axis=0)
        return pltpu.roll(a, size - block, 1)

    return lax.fori_loop(0, size // block, step, matrix)


def kernel(
    gx,
    gy,
    rows,
    faces_hbm,
    edges_hbm,
    fcnt,
    ecnt,
    schur_hbm,
    basis_hbm,
    cmat_hbm,
    l1_hbm,
    l2_hbm,
    outf_hbm,
    oute_hbm,
    faces,
    edges,
    schur,
    basis,
    cmat,
    l1,
    l2,
    rf,
    e1,
    e2,
    e3,
    cs,
    res,
    acc,
    corr,
    out,
    mpart,
    mslots,
    mfull,
    bpart,
    bslots,
    bfull,
    local_sem,
    fsend,
    frecv,
    esend,
    erecv,
    csend,
    crecv,
    osem,
):
    i = lax.axis_index("gx")
    j = lax.axis_index("gy")
    fr = faces.shape[1]
    er = edges.shape[1]
    half = er // 2
    nc = mpart.shape[0]
    owners = nc // rows

    locals_ = [
        pltpu.make_async_copy(src, dst, local_sem.at[n])
        for n, (src, dst) in enumerate(
            (
                (l1_hbm, l1),
                (l2_hbm, l2),
                (cmat_hbm, cmat),
                (edges_hbm, edges),
                (faces_hbm, faces),
                (basis_hbm, basis),
                (schur_hbm, schur),
            )
        )
    ]
    for copy in locals_:
        copy.start()

    has = {-1: i > 0, 1: i < gx - 1}
    hasy = {-1: j > 0, 1: j < gy - 1}

    def peer(d):
        return lax.rem(j + d, gy)

    barrier = pltpu.get_barrier_semaphore()
    for d in range(1, gy):
        pl.semaphore_signal(barrier, inc=1, device_id=(i, peer(d)), device_id_type=MESH)
    for a in (-1, 1):

        @pl.when(has[a])
        def _():
            pl.semaphore_signal(barrier, inc=1, device_id=(i + a, j), device_id_type=MESH)

    pl.semaphore_wait(barrier, gy - 1 + has[-1].astype(jnp.int32) + has[1].astype(jnp.int32))

    def remote(src, dst, ssem, rsem, target):
        return pltpu.make_async_remote_copy(
            src_ref=src,
            dst_ref=dst,
            send_sem=ssem,
            recv_sem=rsem,
            device_id=target,
            device_id_type=MESH,
        )

    def face_has(k):
        a, b = FACE_STEP[k]
        return has[a] if a else hasy[b]

    def face_copy(ph, k, src):
        a, b = FACE_STEP[k]
        return remote(src, rf.at[ph, 3 - k], fsend.at[ph, k], frecv.at[ph, 3 - k], (i + a, j + b))

    def face_arrival(ph, k):
        a, b = FACE_STEP[k]
        return remote(rf.at[ph, k], rf.at[ph, k], fsend.at[ph, k], frecv.at[ph, k], (i + a, j + b))

    def edge_has(s):
        a, b = EDGE_STEP[s]
        return has[a] & hasy[b]

    def mine(s):
        return 0 if s % 2 else half

    def edge_copy(ph, stage, s, src):
        a, b = EDGE_STEP[s]
        land, flip, target = (
            (e1, s ^ 1, (i, j + b)),
            (e2, s ^ 2, (i + a, j)),
            (e3, s ^ 1, (i, j + b)),
        )[stage]
        return remote(
            src, land.at[ph, flip], esend.at[ph, stage, s], erecv.at[ph, stage, flip], target
        )

    def edge_arrival(ph, stage, s):
        a, b = EDGE_STEP[s]
        land = (e1, e2, e3)[stage]
        target = (i + a, j) if stage == 1 else (i, j + b)
        ref = land.at[ph, s]
        return remote(ref, ref, esend.at[ph, stage, s], erecv.at[ph, stage, s], target)

    def owned_by(index):
        return True if owners >= gy else index < owners

    def guarded(cond, fn):
        if cond is True:
            fn()
        else:
            pl.when(cond)(fn)

    def part_rows(ref, index):
        return ref.at[pl.ds(pl.multiple_of(index * rows, rows), rows)]

    def scatter_copy(which, src, slots, d):
        p = peer(d)
        return remote(
            part_rows(src, jnp.minimum(p, owners - 1)), slots.at[d], csend.at[which, d], crecv.at[which, d], (i, p)
        )

    def scatter_start(which, src, slots):
        for d in range(1, gy):
            guarded(owned_by(peer(d)), lambda: scatter_copy(which, src, slots, d).start())

    def gather_copy(which, full, d):
        ref = part_rows(full, jnp.minimum(j, owners - 1))
        return remote(ref, ref, csend.at[which, d], crecv.at[which, d], (i, peer(d)))

    def sum_and_gather(which, src, slots, full):
        def go():
            total = part_rows(src, jnp.minimum(j, owners - 1))[...]
            for d in range(1, gy):
                scatter_copy(which, src, slots, d).wait_recv()
                total = total + slots[d]
            part_rows(full, jnp.minimum(j, owners - 1))[...] = total
            for d in range(1, gy):
                gather_copy(which + 1, full, d).start()

        guarded(owned_by(j), go)

    def gather_wait(which, full):
        for d in range(1, gy):
            q = lax.rem(j - d + gy, gy)

            def wait():
                ref = part_rows(full, jnp.minimum(q, owners - 1))
                remote(ref, ref, csend.at[which, d], crecv.at[which, d], (i, q)).wait_recv()

            guarded(owned_by(q), wait)

    def collective_drain(which, src, slots, full):
        for d in range(1, gy):
            guarded(owned_by(peer(d)), lambda: scatter_copy(which, src, slots, d).wait_send())
            guarded(owned_by(j), lambda: gather_copy(which + 1, full, d).wait_send())

    def edge_halves_start(ph, src):
        for s in range(4):

            @pl.when(edge_has(s))
            def _():
                edge_copy(ph, 0, s, src.at[s, pl.ds(half - mine(s), half)]).start()

    def edge_columns(ph, own):
        for s in range(4):

            @pl.when(edge_has(s))
            def _():
                edge_arrival(ph, 0, s).wait_recv()
                total = own[s, pl.ds(mine(s), half)].astype(F32) + e1[ph, s].astype(F32)
                cs[ph, s] = total.astype(BF16)
                edge_copy(ph, 1, s, cs.at[ph, s]).start()

    def edge_totals(ph, own, dst):
        for s in range(4):
            rows_ref = dst.at[pl.ds(4 * fr + s * er + mine(s), half)]

            @pl.when(edge_has(s))
            def _():
                edge_arrival(ph, 1, s).wait_recv()
                total = own[s, pl.ds(mine(s), half)].astype(F32) + e1[ph, s].astype(F32)
                total = total + e2[ph, s].astype(F32)
                for b in range(half // ROWS):
                    block = mine(s) // ROWS + b
                    scale = jnp.where(ecnt[0, 0, s] > block, 0.25, 0.0)
                    part = total[b * ROWS : (b + 1) * ROWS] * scale
                    rows_ref[pl.ds(b * ROWS, ROWS)] = part.astype(BF16)
                edge_copy(ph, 2, s, rows_ref).start()

    def edge_finish(ph, dst):
        for s in range(4):
            base = 4 * fr + s * er

            @pl.when(edge_has(s))
            def _():
                edge_arrival(ph, 2, s).wait_recv()
                dst[pl.ds(base + half - mine(s), half)] = e3[ph, s]

            @pl.when(jnp.logical_not(edge_has(s)))
            def _():
                dst[pl.ds(base, er)] = jnp.zeros((er, dst.shape[1]), BF16)

    def face_finish(ph, k, own, dst):
        @pl.when(face_has(k))
        def _():
            face_arrival(ph, k).wait_recv()
            for b in range(fr // ROWS):
                scale = jnp.where(fcnt[0, 0, k] > b, 0.5, 0.0)
                at = pl.ds(b * ROWS, ROWS)
                total = own[k, at].astype(F32) + rf[ph, k, at].astype(F32)
                dst[pl.ds(k * fr + b * ROWS, ROWS)] = (total * scale).astype(BF16)

        @pl.when(jnp.logical_not(face_has(k)))
        def _():
            dst[pl.ds(k * fr, fr)] = jnp.zeros((fr, dst.shape[1]), BF16)

    edge_halves_start(0, edges_hbm)
    for k in (0, 3, 1, 2):

        @pl.when(face_has(k))
        def _():
            face_copy(0, k, faces_hbm.at[k]).start()

    for n in range(3):
        locals_[n].wait()
    lift = exact_dot(l1[...], l2[...])
    l1[...] = lift
    mpart[...] = exact_dot_t(lift, exact_dot(cmat[...], lift))
    scatter_start(0, mpart, mslots)
    locals_[3].wait()
    edge_columns(0, edges)
    sum_and_gather(0, mpart, mslots, mfull)
    gather_wait(1, mfull)
    mfull_inv = invert(mfull[...])
    collective_drain(0, mpart, mslots, mfull)
    l2[...] = mfull_inv

    locals_[4].wait()
    for k in (1, 2):
        face_finish(0, k, faces, res)
    edge_totals(0, edges, res)
    for k in (0, 3):
        face_finish(0, k, faces, res)
    edge_finish(0, res)

    locals_[5].wait()
    coarse = lax.dot_general(basis[...], res[...], COLS0, preferred_element_type=F32)
    bpart[...] = exact_dot_t(l1[...], coarse)
    scatter_start(2, bpart, bslots)
    locals_[6].wait()

    def local_solve(base, count):
        at = pl.ds(pl.multiple_of(base, 128), count)
        acc[at] = jnp.dot(schur[at], res[...], preferred_element_type=F32)

    @pl.loop(0, 2)
    def _(t):
        local_solve(t * (3 * fr), fr)

    sum_and_gather(2, bpart, bslots, bfull)

    @pl.loop(0, 3)
    def _(t):
        local_solve(jnp.where(t == 0, 4 * fr, t * fr), fr)

    local_solve(5 * fr, 4 * er - fr)

    gather_wait(3, bfull)
    middle = exact_dot(l2[...], bfull[...])
    node = exact_dot(l1[...], middle).astype(BF16)

    def add_coarse(base, count):
        at = pl.ds(base, count)
        return (acc[at] + jnp.dot(basis[at], node, preferred_element_type=F32)).astype(BF16)

    for s in range(4):
        edges[s] = add_coarse(4 * fr + s * er, er)
    for k in (0, 3, 1, 2):
        corr[k] = add_coarse(k * fr, fr)
        if k == 0:
            for s in range(4):

                @pl.when(edge_has(s))
                def _():
                    edge_copy(0, 0, s, edges_hbm.at[s, pl.ds(half - mine(s), half)]).wait_send()

            edge_halves_start(1, edges)

        @pl.when(face_has(k))
        def _():
            face_copy(1, k, corr.at[k]).start()

    edge_columns(1, edges)

    def put_face(k):
        return pltpu.make_async_copy(out.at[pl.ds(k * fr, fr)], outf_hbm.at[k], osem.at[k])

    def put_edge(s):
        return pltpu.make_async_copy(
            out.at[pl.ds(4 * fr + s * er, er)], oute_hbm.at[s], osem.at[4 + s]
        )

    for k in (1, 2):
        face_finish(1, k, corr, out)
        put_face(k).start()
    edge_totals(1, edges, out)
    for k in (0, 3):
        face_finish(1, k, corr, out)
        put_face(k).start()
    edge_finish(1, out)
    for s in range(4):
        put_edge(s).start()

    collective_drain(2, bpart, bslots, bfull)
    for ph in range(2):
        for k in range(4):

            @pl.when(face_has(k))
            def _():
                face_copy(ph, k, faces_hbm.at[k] if ph == 0 else corr.at[k]).wait_send()

        for s in range(4):

            @pl.when(edge_has(s))
            def _():
                if ph:
                    edge_copy(1, 0, s, edges.at[s, pl.ds(half - mine(s), half)]).wait_send()
                edge_copy(ph, 1, s, cs.at[ph, s]).wait_send()
                edge_copy(
                    ph, 2, s, (out if ph else res).at[pl.ds(4 * fr + s * er + mine(s), half)]
                ).wait_send()

    for k in range(4):
        put_face(k).wait()
        put_edge(k).wait()


def body(
    face_pieces,
    edge_pieces,
    face_counts,
    edge_counts,
    schur_inv,
    coarse_basis,
    coarse_mat,
    lift_one,
    lift_two,
):
    gx, gy = lax.axis_size("gx"), lax.axis_size("gy")
    faces, edges = face_pieces[0, 0], edge_pieces[0, 0]
    fr, vec = faces.shape[1:]
    er = edges.shape[1]
    ni, nc = coarse_basis.shape[2:]
    rows = max(16, nc // gy)
    half = er // 2
    anywhere = pl.BlockSpec(memory_space=pl.ANY)
    smem = pl.BlockSpec(memory_space=pltpu.SMEM)
    dma = pltpu.SemaphoreType.DMA
    out_faces, out_edges = pl.pallas_call(
        functools.partial(kernel, gx, gy, rows),
        out_shape=(
            jax.ShapeDtypeStruct(faces.shape, BF16),
            jax.ShapeDtypeStruct(edges.shape, BF16),
        ),
        in_specs=[anywhere, anywhere, smem, smem] + [anywhere] * 5,
        out_specs=(anywhere, anywhere),
        scratch_shapes=[
            pltpu.VMEM(faces.shape, BF16),
            pltpu.VMEM(edges.shape, BF16),
            pltpu.VMEM((ni, ni), BF16),
            pltpu.VMEM((ni, nc), BF16),
            pltpu.VMEM((nc, nc), F32),
            pltpu.VMEM((nc, nc), F32),
            pltpu.VMEM((nc, nc), F32),
            pltpu.VMEM((2, 4, fr, vec), BF16),
            pltpu.VMEM((2, 4, half, vec), BF16),
            pltpu.VMEM((2, 4, half, vec), BF16),
            pltpu.VMEM((2, 4, half, vec), BF16),
            pltpu.VMEM((2, 4, half, vec), BF16),
            pltpu.VMEM((ni, vec), BF16),
            pltpu.VMEM((ni, vec), F32),
            pltpu.VMEM(faces.shape, BF16),
            pltpu.VMEM((ni, vec), BF16),
            pltpu.VMEM((nc, nc), F32),
            pltpu.VMEM((gy, rows, nc), F32),
            pltpu.VMEM((nc, nc), F32),
            pltpu.VMEM((nc, vec), F32),
            pltpu.VMEM((gy, rows, vec), F32),
            pltpu.VMEM((nc, vec), F32),
            dma((7,)),
            dma((2, 4)),
            dma((2, 4)),
            dma((2, 3, 4)),
            dma((2, 3, 4)),
            dma((4, gy)),
            dma((4, gy)),
            dma((8,)),
        ],
        compiler_params=pltpu.CompilerParams(
            collective_id=0, has_side_effects=True, vmem_limit_bytes=52 * 2**20
        ),
        cost_estimate=pl.CostEstimate(
            flops=2 * ni * vec * (ni + 2 * nc), bytes_accessed=2 * ni * (ni + 3 * vec), transcendentals=0
        ),
    )(
        faces,
        edges,
        face_counts,
        edge_counts,
        schur_inv[0, 0],
        coarse_basis[0, 0],
        coarse_mat[0, 0],
        lift_one[0, 0],
        lift_two[0, 0],
    )
    return out_faces[None, None], out_edges[None, None]


def solution(mesh):
    return jax.shard_map(
        body,
        mesh=mesh,
        in_specs=(
            P("gx", "gy", None, None, None),
            P("gx", "gy", None, None, None),
            P("gx", "gy", None),
            P("gx", "gy", None),
            P("gx", "gy", None, None),
            P("gx", "gy", None, None),
            P("gx", "gy", None, None),
            P("gx", "gy", None, None),
            P("gx", "gy", None, None),
        ),
        out_specs=(P("gx", "gy", None, None, None), P("gx", "gy", None, None, None)),
        check_vma=False,
    )
```

time: 153 us -> 85.7 us (0.56)
  Pallas kernels: 0 us -> 75.3 us
  starting transfers between devices: 64 us -> 0 us
  other arithmetic: 39.1 us -> 0 us
  waiting for transfers between devices: 15.1 us -> 0 us
  matrix products: 13.4 us -> 0 us
  local copies, waits for them, and re-layouts: 19.1 us -> 9.35 us
    pallas_call x0 -> x1, Pallas kernels: none -> 75.3 us  [body(): pl.pallas_call(functools.partial(kernel, gx, gy, rows), out_shape=(jax.Sh...]
    ppermute x24 -> x0, starting transfers between devices: 64 us -> none  [the longest x20 62 us: from_behind(): lax.ppermute(value, axis, [(source, source + steps) for source in range(f...]
    another operation x16 -> x0, other arithmetic: 30.2 us -> none  [the longest x3 12.4 us: body(): factor = jnp.linalg.cholesky(row_total[:, :coarse_size])]
    ppermute x24 -> x0, waiting for transfers between devices: 15.1 us -> none  [the longest x4 12.8 us: from_partner(): return lax.ppermute(value, axis, pairs)]
    dot_general x11 -> x0, matrix products: 12.6 us -> none  [the longest x1 6.17 us: body(): jnp.dot(schur_inv[0, 0], flat_rhs, preferred_element_type=jnp.float32)]
    convert_element_type x7 -> x0, other arithmetic: 7.34 us -> none  [the longest x1 3.68 us: body(): (face_out * 0.5 * face_live).astype(jnp.bfloat16)[None, None]]
    slice x15 -> x0, local copies, waits for them, and re-layouts: 7.25 us -> none  [the longest x6 3.84 us: neighbour_sum(): row_edges[offset] = from_behind(edges[first:first + 2], 'gx', offset)]
    convert_element_type x3 -> x0, local copies, waits for them, and re-layouts: 7.12 us -> none  [the longest x2 7.11 us: widen(): return values.astype(jnp.float32)]
  transfers between devices with their start and end apart: 24 -> 0, of which waited for: 6 -> 0; matrix products, arithmetic and copies ran while one was open for 21% -> 0% of each run, Pallas kernels for 0% -> 0%
where the time goes in v1:
time: 85.7 us; the launch traced here: 85.3 us
  Pallas kernels  75.3 us (88%)
  local copies, waits for them, and re-layouts  9.35 us (11%)
    pallas_call x1, Pallas kernels, body(): pl.pallas_call(functools.partial(kernel, gx, gy, rows), out_shape=(jax.Sh...  75.3 us
    unnamed x16, local copies, waits for them, and re-layouts  9.35 us

profile of v1, /device:TPU:11, one launch (start us, length us, event | category | flops | bytes accessed | tf_op | source)
XLA Modules:
  0.0 85.3 jit_solution(1254235881854464018)
XLA Ops:
  0.6 0.0 copy-start
  0.6 1.0 %copy-done = bf16[1,1,4,128,512]{4,3,2,1,0:T(8,128)(2,1)S(1)} copy-done((bf16[1,1,4,128,512]{4,3,2,1,0:T(8,128)(2,1)S(1)}, bf16[1,1,4,128,512]{4,3,2,1,0:T(8,128)(2,1)}, u32[]{:S(2)}) %copy-start) | copy-done | bytes 524312
  1.7 0.0 copy-start.1
  1.7 1.0 %copy-done.1 = bf16[1,1,2048,128]{3,2,1,0:T(8,128)(2,1)S(1)} copy-done((bf16[1,1,2048,128]{3,2,1,0:T(8,128)(2,1)S(1)}, bf16[1,1,2048,128]{3,2,1,0:T(8,128)(2,1)}, u32[]{:S(2)}) %copy-start.1) | copy-done | bytes 524312
  2.7 0.0 copy-start.2
  2.7 0.8 copy-done.2
  3.6 0.0 copy-start.3
  3.6 0.8 copy-done.3
  4.4 0.0 copy-start.4
  4.4 0.8 copy-done.4
  5.2 0.0 copy-start.5
  5.2 0.7 copy-done.5
  5.9 0.0 copy-start.6
  5.9 0.7 copy-done.6
  6.5 75.3 %shard_map.104 = (bf16[4,384,512]{2,1,0:T(8,128)(2,1)}, bf16[4,128,512]{2,1,0:T(8,128)(2,1)S(1)}) custom-call(bf16[4,384,512]{2,1,0:T(8,128)(2,1)} %bitcast.17, bf16[4,128,512]{2,1,0:T(8,128)(2,1)S(1)} %bitcast.10, s32[1,1,4]{2,1,0:T(1,128)S(1)} %copy-done.5, s32[1,1,4]{2,1,0:T(1,128)S(1)} %copy-done.6, bf16[2048,2048]{1,0:T(8,128)(2,1)} %bitcast.16, ...), custom_call_target="tpu_custom_call" | custom-call | flops 4831838208 | bytes 14680064 | tf_op jit(solution)/shard_map/pallas_call | solution.py:449
  81.9 2.7 %copy.13 = bf16[1,1,4,384,512]{4,3,2,1,0:T(8,128)(2,1)} copy(bf16[1,1,4,384,512]{4,3,2,1,0:T(8,128)(2,1)} %bitcast.15) | data formatting | bytes 3145728
  84.5 0.8 copy.14
Async XLA Ops:
  0.6 1.0 %copy-start = (bf16[1,1,4,128,512]{4,3,2,1,0:T(8,128)(2,1)S(1)}, bf16[1,1,4,128,512]{4,3,2,1,0:T(8,128)(2,1)}, u32[]{:S(2)}) copy-start(bf16[1,1,4,128,512]{4,3,2,1,0:T(8,128)(2,1)} %param.10) | copy-start | bytes 1572868
  1.7 1.0 %copy-start.1 = (bf16[1,1,2048,128]{3,2,1,0:T(8,128)(2,1)S(1)}, bf16[1,1,2048,128]{3,2,1,0:T(8,128)(2,1)}, u32[]{:S(2)}) copy-start(bf16[1,1,2048,128]{3,2,1,0:T(8,128)(2,1)} %param.14) | copy-start | bytes 1572868
  2.7 0.8 copy-start.2
  3.6 0.8 copy-start.3
  4.4 0.8 copy-start.4
  5.2 0.7 copy-start.5
  5.9 0.7 copy-start.6

commit v2 on v1

--- a/solution.py
+++ b/solution.py
@@ -29,29 +29,32 @@
     size = matrix.shape[0]
     block = 8
     lane = lax.broadcasted_iota(jnp.int32, (1, size), 1)
-    row = lax.broadcasted_iota(jnp.int32, (size, 1), 0)
 
     def step(_, a):
+        cols = [jnp.broadcast_to(a[:, t : t + 1], (size, size)) for t in range(block)]
+        d = [[cols[t][s : s + 1] for t in range(block)] for s in range(block)]
+        w = [
+            jnp.where(lane < block, jnp.where(lane == s, 1.0, 0.0), a[s : s + 1])
+            for s in range(block)
+        ]
         for p in range(0, block, 2):
             q = p + 1
-            r0, r1 = a[p : p + 1, :], a[q : q + 1, :]
-            c0, c1 = a[:, p : p + 1], a[:, q : q + 1]
-            d00, d01 = a[p : p + 1, p : p + 1], a[p : p + 1, q : q + 1]
-            d10, d11 = a[q : q + 1, p : p + 1], a[q : q + 1, q : q + 1]
-            inv = 1.0 / (d00 * d11 - d01 * d10)
-            e0 = jnp.where(lane == p, 1.0, 0.0)
-            e1 = jnp.where(lane == q, 1.0, 0.0)
-            pivot_lane = (lane == p) | (lane == q)
-            pivot_row = (row == p) | (row == q)
-            r0 = jnp.where(pivot_lane, e0, r0)
-            r1 = jnp.where(pivot_lane, e1, r1)
-            w0 = (d11 * inv) * r0 - (d01 * inv) * r1
-            w1 = (d00 * inv) * r1 - (d10 * inv) * r0
-            c0 = jnp.where(pivot_row, jnp.where(row == p, -1.0, 0.0), c0)
-            c1 = jnp.where(pivot_row, jnp.where(row == q, -1.0, 0.0), c1)
-            a = jnp.where(pivot_row | pivot_lane, 0.0, a) - c0 * w0 - c1 * w1
-        a = jnp.concatenate([a[block:], a[:block]], axis=0)
-        return pltpu.roll(a, size - block, 1)
+            inv = 1.0 / (d[p][p] * d[q][q] - d[p][q] * d[q][p])
+            i00, i01 = d[q][q] * inv, d[p][q] * inv
+            i10, i11 = d[q][p] * inv, d[p][p] * inv
+            w[p], w[q] = i00 * w[p] - i01 * w[q], i11 * w[q] - i10 * w[p]
+            for t in range(q + 1, block):
+                d[p][t], d[q][t] = i00 * d[p][t] - i01 * d[q][t], i11 * d[q][t] - i10 * d[p][t]
+            for s in range(block):
+                if s not in (p, q):
+                    f, g = d[s][p], d[s][q]
+                    w[s] = w[s] - f * w[p] - g * w[q]
+                    for t in range(q + 1, block):
+                        d[s][t] = d[s][t] - f * d[p][t] - g * d[q][t]
+        rest = jnp.where(lane < block, 0.0, a[block:])
+        for t in range(block):
+            rest = rest - cols[t][block:] * w[t]
+        return pltpu.roll(jnp.concatenate([rest] + w, axis=0), size - block, 1)
 
     return lax.fori_loop(0, size // block, step, matrix)
 
@@ -487,7 +490,7 @@
             dma((8,)),
         ],
         compiler_params=pltpu.CompilerParams(
-            collective_id=0, has_side_effects=True, vmem_limit_bytes=52 * 2**20
+            collective_id=0, has_side_effects=True, vmem_limit_bytes=62 * 2**20
         ),
         cost_estimate=pl.CostEstimate(
             flops=2 * ni * vec * (ni + 2 * nc), bytes_accessed=2 * ni * (ni + 3 * vec), transcendentals=0

time: 85.7 us -> 64.7 us (0.75)
  Pallas kernels: 75.3 us -> 60.4 us
  local copies, waits for them, and re-layouts: 9.35 us -> 3.51 us
    pallas_call x1, Pallas kernels: 75.3 us -> 60.4 us  [body(): pl.pallas_call(functools.partial(kernel, gx, gy, rows), out_shape=(jax.Sh...]
    unnamed x16 -> x4, local copies, waits for them, and re-layouts: 9.35 us -> 3.51 us
where the time goes in v2:
time: 64.7 us; the launch traced here: 64.5 us
  Pallas kernels  60.4 us (93%)
  local copies, waits for them, and re-layouts  3.51 us (5%)
  between operations  0.65 us (1%)
    pallas_call x1, Pallas kernels, body(): pl.pallas_call(functools.partial(kernel, gx, gy, rows), out_shape=(jax.Sh...  60.4 us
    unnamed x4, local copies, waits for them, and re-layouts  3.51 us

profile of v2, /device:TPU:11, one launch (start us, length us, event | category | flops | bytes accessed | tf_op | source)
XLA Modules:
  0.0 64.5 jit_solution(8239530646956988312)
XLA Ops:
  0.6 60.4 %shard_map.104 = (bf16[4,384,512]{2,1,0:T(8,128)(2,1)}, bf16[4,128,512]{2,1,0:T(8,128)(2,1)}) custom-call(bf16[4,384,512]{2,1,0:T(8,128)(2,1)} %bitcast.12, bf16[4,128,512]{2,1,0:T(8,128)(2,1)} %bitcast.13, s32[1,1,4]{2,1,0:T(1,128)} %fcnt.1, s32[1,1,4]{2,1,0:T(1,128)} %ecnt.1, bf16[2048,2048]{1,0:T(8,128)(2,1)} %bitcast.11, bf16[2048,128]{1,0:T(8,128)(2,1)} %bitcast.14, ...), custom_call_target="tpu_custom_call" | custom-call | flops 4831838208 | bytes 14680064 | tf_op jit(solution)/shard_map/pallas_call | solution.py:452
  61.0 0.0 copy-start
  61.0 2.7 %copy.13 = bf16[1,1,4,384,512]{4,3,2,1,0:T(8,128)(2,1)} copy(bf16[1,1,4,384,512]{4,3,2,1,0:T(8,128)(2,1)} %bitcast.9) | data formatting | bytes 3145728
  63.7 0.0 copy-done
  63.7 0.8 %copy.14 = bf16[1,1,4,128,512]{4,3,2,1,0:T(8,128)(2,1)} copy(bf16[1,1,4,128,512]{4,3,2,1,0:T(8,128)(2,1)S(1)} %bitcast.10) | data formatting | bytes 1048576
Async XLA Ops:
  61.0 2.7 %copy-start = (bf16[4,128,512]{2,1,0:T(8,128)(2,1)S(1)}, bf16[4,128,512]{2,1,0:T(8,128)(2,1)}, u32[]{:S(2)}) copy-start(bf16[4,128,512]{2,1,0:T(8,128)(2,1)} %get-tuple-element.5) | copy-start | bytes 1572868

commit v3 on v2

--- a/solution.py
+++ b/solution.py
@@ -308,11 +308,14 @@
             dst[pl.ds(k * fr, fr)] = jnp.zeros((fr, dst.shape[1]), BF16)
 
     edge_halves_start(0, edges_hbm)
-    for k in (0, 3, 1, 2):
-
-        @pl.when(face_has(k))
-        def _():
-            face_copy(0, k, faces_hbm.at[k]).start()
+    def pieces_start(ks):
+        for k in ks:
+
+            @pl.when(face_has(k))
+            def _():
+                face_copy(0, k, faces_hbm.at[k]).start()
+
+    pieces_start((0, 3))
 
     for n in range(3):
         locals_[n].wait()
@@ -323,16 +326,15 @@
     locals_[3].wait()
     edge_columns(0, edges)
     sum_and_gather(0, mpart, mslots, mfull)
+    pieces_start((1, 2))
     gather_wait(1, mfull)
     mfull_inv = invert(mfull[...])
     collective_drain(0, mpart, mslots, mfull)
     l2[...] = mfull_inv
 
     locals_[4].wait()
-    for k in (1, 2):
-        face_finish(0, k, faces, res)
     edge_totals(0, edges, res)
-    for k in (0, 3):
+    for k in (0, 3, 1, 2):
         face_finish(0, k, faces, res)
     edge_finish(0, res)
 

time: 64.7 us -> 56.8 us (0.88)
  Pallas kernels: 60.4 us -> 52.5 us
    pallas_call x1, Pallas kernels: 60.4 us -> 52.5 us  [body(): pl.pallas_call(functools.partial(kernel, gx, gy, rows), out_shape=(jax.Sh...]
where the time goes in v3:
time: 56.8 us; the launch traced here: 56.7 us
  Pallas kernels  52.5 us (92%)
  local copies, waits for them, and re-layouts  3.51 us (6%)
  between operations  0.65 us (1%)
    pallas_call x1, Pallas kernels, body(): pl.pallas_call(functools.partial(kernel, gx, gy, rows), out_shape=(jax.Sh...  52.5 us
    unnamed x4, local copies, waits for them, and re-layouts  3.51 us

profile of v3, /device:TPU:11, one launch (start us, length us, event | category | flops | bytes accessed | tf_op | source)
XLA Modules:
  0.0 56.7 jit_solution(7544141797310768754)
XLA Ops:
  0.6 52.5 %shard_map.104 = (bf16[4,384,512]{2,1,0:T(8,128)(2,1)}, bf16[4,128,512]{2,1,0:T(8,128)(2,1)}) custom-call(bf16[4,384,512]{2,1,0:T(8,128)(2,1)} %bitcast.12, bf16[4,128,512]{2,1,0:T(8,128)(2,1)} %bitcast.13, s32[1,1,4]{2,1,0:T(1,128)} %fcnt.1, s32[1,1,4]{2,1,0:T(1,128)} %ecnt.1, bf16[2048,2048]{1,0:T(8,128)(2,1)} %bitcast.11, bf16[2048,128]{1,0:T(8,128)(2,1)} %bitcast.14, ...), custom_call_target="tpu_custom_call" | custom-call | flops 4831838208 | bytes 14680064 | tf_op jit(solution)/shard_map/pallas_call | solution.py:454
  53.1 0.0 copy-start
  53.1 2.7 %copy.13 = bf16[1,1,4,384,512]{4,3,2,1,0:T(8,128)(2,1)} copy(bf16[1,1,4,384,512]{4,3,2,1,0:T(8,128)(2,1)} %bitcast.9) | data formatting | bytes 3145728
  55.9 0.0 copy-done
  55.9 0.8 %copy.14 = bf16[1,1,4,128,512]{4,3,2,1,0:T(8,128)(2,1)} copy(bf16[1,1,4,128,512]{4,3,2,1,0:T(8,128)(2,1)S(1)} %bitcast.10) | data formatting | bytes 1048576
Async XLA Ops:
  53.1 2.7 %copy-start = (bf16[4,128,512]{2,1,0:T(8,128)(2,1)S(1)}, bf16[4,128,512]{2,1,0:T(8,128)(2,1)}, u32[]{:S(2)}) copy-start(bf16[4,128,512]{2,1,0:T(8,128)(2,1)} %get-tuple-element.5) | copy-start | bytes 1572868

commit v4 on v3

--- a/solution.py
+++ b/solution.py
@@ -330,7 +330,7 @@
     gather_wait(1, mfull)
     mfull_inv = invert(mfull[...])
     collective_drain(0, mpart, mslots, mfull)
-    l2[...] = mfull_inv
+    l2[...] = exact_dot(l1[...], mfull_inv)
 
     locals_[4].wait()
     edge_totals(0, edges, res)
@@ -361,8 +361,7 @@
     local_solve(5 * fr, 4 * er - fr)
 
     gather_wait(3, bfull)
-    middle = exact_dot(l2[...], bfull[...])
-    node = exact_dot(l1[...], middle).astype(BF16)
+    node = exact_dot(l2[...], bfull[...]).astype(BF16)
 
     def add_coarse(base, count):
         at = pl.ds(base, count)

time: 56.8 us -> 56.7 us (level)
  no operation moved by 1% of the time
where the time goes in v4:
time: 56.7 us; the launch traced here: 56.5 us
  Pallas kernels  52.4 us (92%)
  local copies, waits for them, and re-layouts  3.51 us (6%)
  between operations  0.65 us (1%)
    pallas_call x1, Pallas kernels, body(): pl.pallas_call(functools.partial(kernel, gx, gy, rows), out_shape=(jax.Sh...  52.4 us
    unnamed x4, local copies, waits for them, and re-layouts  3.51 us

profile of v4, /device:TPU:11, one launch (start us, length us, event | category | flops | bytes accessed | tf_op | source)
XLA Modules:
  0.0 56.5 jit_solution(15286411256850955089)
XLA Ops:
  0.6 52.4 %shard_map.104 = (bf16[4,384,512]{2,1,0:T(8,128)(2,1)}, bf16[4,128,512]{2,1,0:T(8,128)(2,1)}) custom-call(bf16[4,384,512]{2,1,0:T(8,128)(2,1)} %bitcast.12, bf16[4,128,512]{2,1,0:T(8,128)(2,1)} %bitcast.13, s32[1,1,4]{2,1,0:T(1,128)} %fcnt.1, s32[1,1,4]{2,1,0:T(1,128)} %ecnt.1, bf16[2048,2048]{1,0:T(8,128)(2,1)} %bitcast.11, bf16[2048,128]{1,0:T(8,128)(2,1)} %bitcast.14, ...), custom_call_target="tpu_custom_call" | custom-call | flops 4831838208 | bytes 14680064 | tf_op jit(solution)/shard_map/pallas_call | solution.py:453
  53.0 0.0 copy-start
  53.0 2.7 %copy.13 = bf16[1,1,4,384,512]{4,3,2,1,0:T(8,128)(2,1)} copy(bf16[1,1,4,384,512]{4,3,2,1,0:T(8,128)(2,1)} %bitcast.9) | data formatting | bytes 3145728
  55.7 0.0 copy-done
  55.8 0.8 %copy.14 = bf16[1,1,4,128,512]{4,3,2,1,0:T(8,128)(2,1)} copy(bf16[1,1,4,128,512]{4,3,2,1,0:T(8,128)(2,1)S(1)} %bitcast.10) | data formatting | bytes 1048576
Async XLA Ops:
  53.0 2.7 %copy-start = (bf16[4,128,512]{2,1,0:T(8,128)(2,1)S(1)}, bf16[4,128,512]{2,1,0:T(8,128)(2,1)}, u32[]{:S(2)}) copy-start(bf16[4,128,512]{2,1,0:T(8,128)(2,1)} %get-tuple-element.5) | copy-start | bytes 1572868
